TPU v7x, 32 devices: a whole 2x2x4 slice. The times are simulated.
32 devices in a mesh: row: 8 (over z, y), col: 4 (over x, core).
Axes of the slice: x: 2, y: 2, z: 4, core: 2. Of those that a mesh axis runs over, the one named last changes fastest.
Arguments:
- factors: bfloat16 [768, 12, 5120], P('row', None, 'col'), may hold values from -0.21875 to 0.21875
- amplitudes: bfloat16 [4, 12, 12], replicated, may hold values from -6 to 6
- vir_energy: float32 [768], replicated, may hold values from 0.2 to 2
- pair_energy: float32 [4], replicated, may hold values from -1.5 to -0.5
Outputs:
- residual: float32 [4, 768, 768], P('col', 'row')
- update: float32 [4, 768, 768], P('col', 'row')
All inputs are finite; a program needn't handle non-finite values.
Results may differ from a plain program's by a relative error of at most 0.0024.
Values may be sent and summed in bfloat16 or wider, within the bound.
A program may use at most 256 MiB of HBM per device.

v0:
```python
import jax
import jax.numpy as jnp
from jax import lax
from jax.sharding import PartitionSpec as P


def block_terms(left_side, shard_piece, row_count):
    piece_rows = shard_piece.shape[0]
    slab_size = shard_piece.shape[1]
    products = lax.dot_general(
        left_side,
        shard_piece.reshape(piece_rows * slab_size, -1),
        (((1,), (1,)), ((), ())),
        preferred_element_type=jnp.float32,
    )
    return products.astype(jnp.bfloat16).reshape(row_count, slab_size, piece_rows, slab_size)


def own_term(products, amplitudes):
    return jnp.einsum("acbd,pcd->pab", products, amplitudes, preferred_element_type=jnp.float32)


def mirror_term(products, amplitudes):
    return jnp.einsum("bdac,pcd->pab", products, amplitudes, preferred_element_type=jnp.float32)


def per_device(factors, amplitudes, vir_energy, pair_energy):
    row_count, slab_size, aux_count = factors.shape
    pair_count = amplitudes.shape[0]
    vir_total = vir_energy.shape[0]
    row_devices = lax.axis_size("row")
    here_row = lax.axis_index("row")
    here_col = lax.axis_index("col")
    left_side = factors.reshape(row_count * slab_size, aux_count)
    partial_rows = jnp.zeros((pair_count, row_count, vir_total), jnp.float32)
    outgoing = jnp.zeros((pair_count, row_count, row_devices, row_count), jnp.float32)
    gathered = lax.all_gather(factors, "row", axis=0, tiled=True)

    def visit_lower(other_row, state_tuple):
        partial_sum, sending = state_tuple
        current = lax.dynamic_slice_in_dim(gathered, other_row * row_count, row_count, 0)
        products = block_terms(left_side, current, row_count)
        own_block = own_term(products, amplitudes)
        partial_sum = lax.dynamic_update_slice_in_dim(
            partial_sum, own_block, other_row * row_count, 2
        )
        mirror = mirror_term(products, amplitudes) * jnp.where(
            other_row < here_row, 1.0, 0.0
        ).astype(jnp.float32)
        sending = lax.dynamic_update_slice_in_dim(sending, mirror[:, :, None, :], other_row, 2)
        return (partial_sum, sending)

    partial_rows, outgoing = lax.fori_loop(0, here_row + 1, visit_lower, (partial_rows, outgoing))
    received = lax.all_to_all(outgoing, "row", split_axis=2, concat_axis=2, tiled=True)
    row_sum = partial_rows + received.reshape(pair_count, row_count, vir_total)
    reduced = lax.psum_scatter(row_sum, "col", scatter_dimension=0, tiled=True)
    pair_share = reduced.shape[0]
    first_energy = lax.dynamic_slice_in_dim(vir_energy, here_row * row_count, row_count)
    pair_here = lax.dynamic_slice_in_dim(pair_energy, here_col * pair_share, pair_share)
    divisor = first_energy[None, :, None] + vir_energy[None, None, :] - pair_here[:, None, None]
    return (reduced, reduced / divisor)


def solution(mesh):
    return jax.shard_map(
        per_device,
        mesh=mesh,
        in_specs=(P("row", None, "col"), P(), P(), P()),
        out_specs=(P("col", "row", None), P("col", "row", None)),
        check_vma=False,
    )
```

profile of v0, /device:TPU:0, one launch (start us, length us, event | category | flops | bytes accessed | tf_op | source)
XLA Modules:
  0.0 1469.6 jit_solution(11776488615706446198)
XLA Ops:
  7.2 0.0 copy-start
  7.2 0.0 all-gather.2.cloned.1.call-start
  7.2 0.7 all-gather.2.cloned.1.call-update
  7.9 0.0 reduce-scatter.2.cloned.1.call-start
  8.0 1.0 copy-done
  9.0 3.5 copy.23
  12.5 0.0 copy-start.2
  12.5 5.6 reshape.71
  18.1 0.0 copy-done.2
  18.1 0.1 copy.25
  18.3 445.0 %all-gather.2.cloned.1.call-done = bf16[768,12,1280]{2,0,1:T(8,128)(2,1)} async-done(((bf16[96,12,1280]{2,0,1:T(8,128)(2,1)}), bf16[768,12,1280]{2,0,1:T(8,128)(2,1)}) %all-gather.2.cloned.1.call-update) | async-done | bytes 23592976 | tf_op jit(solution)/shard_map/all_gather | solution.py:37
  463.2 1.4 broadcast_in_dim.13
  464.6 1.1 broadcast_in_dim.12.clone
  465.8 115.0 %while.12 = (s32[]{:T(128)}, f32[4,96,768]{2,1,0:T(8,128)}, f32[4,96,8,96]{1,0,3,2:T(4,128)}, s32[]{:T(128)}, bf16[768,12,1280]{2,0,1:T(8,128)(2,1)}, /*index=5*...) while((s32[]{:T(128)}, f32[4,96,768]{2,1,0:T(8,128)}, ...), condition=%wide.region_1.2_spmd, body=%wide.region_0.1_spmd.sunk | while | flops 3419983872 | bytes 68768512 | solution.py:53
  465.8 2.0 constant_dynamic-slice_fusion.2
  467.8 3.5 copy.40
  471.3 3.9 reshape.79
  475.2 7.1 fusion.24
  482.4 4.1 copy.41
  486.5 65.0 %reshape.80 = bf16[96,12,96,12]{3,2,1,0:T(8,128)(2,1)} reshape(bf16[1152,1152]{1,0:T(8,128)(2,1)S(1)} %copy.41) | data formatting | bytes 5308416 | tf_op jit(solution)/shard_map/while/body/reshape | solution.py:16
  551.5 0.1 copy.42
  551.6 13.3 convolution_bitcast_fusion.3
  565.0 1.8 dynamic_update_slice.10
  566.8 14.0 fusion.25
  580.8 0.0 copy-start.1
  580.8 850.4 %all_to_all.5 = f32[4,96,8,96]{1,0,3,2:T(4,128)S(1)} all-to-all(f32[4,96,8,96]{1,0,3,2:T(4,128)} %get-tuple-element.47), channel_id=1, replica_groups=mesh['row'=8,'col'=4] {'row'}, dimensions={2} | all-to-all | bytes 2359296 | tf_op jit(solution)/shard_map/all_to_all | solution.py:54
  1431.1 1.5 copy.32
  1432.7 0.0 copy-start.3
  1432.7 0.0 copy-start.4
  1432.7 0.0 copy-done.1
  1432.7 2.5 add.46
  1435.1 0.0 reduce-scatter.2.cloned.1.call-update
  1435.2 0.0 copy-done.3
  1435.2 0.1 dynamic_slice.9
  1435.3 0.0 copy-done.4
  1435.3 0.6 dynamic_slice.10
  1435.9 24.4 %reduce-scatter.2.cloned.1.call-done = f32[1,96,768]{2,1,0:T(8,128)} async-done(((f32[4,96,768]{2,1,0:T(8,128)}), f32[1,96,768]{2,1,0:T(8,128)}) %reduce-scatter.2.cloned.1.call-update) | async-done | bytes 294928 | tf_op jit(solution)/shard_map/reduce_scatter | solution.py:56
  1460.3 2.5 subtract_divide_fusion
  (1 shorter events, 0.0 us)
Async XLA Ops:
  7.2 1.8 copy-start
  7.2 456.0 %all-gather.2.cloned.1.call-start = ((), (), s32[]{:S(2)}) async-start(), calls=%async_computation.2 | async-start | bytes 26542080 | tf_op jit(solution)/shard_map/all_gather | solution.py:37
  7.9 1452.4 %reduce-scatter.2.cloned.1.call-start = ((), (), s32[]{:S(2)}) async-start(), calls=%async_computation.3 | async-start | bytes 1474560 | tf_op jit(solution)/shard_map/reduce_scatter | solution.py:56
  12.5 5.6 copy-start.2
  580.8 851.9 %copy-start.1 = (f32[4,96,768]{2,1,0:T(8,128)S(1)}, f32[4,96,768]{2,1,0:T(8,128)}, u32[]{:S(2)}) copy-start(f32[4,96,768]{2,1,0:T(8,128)} %get-tuple-element.46) | copy-start | bytes 3538948
  1432.7 2.5 copy-start.3
  1432.7 2.6 copy-start.4
Sparse Core Ops, SparseCore 0:
  9.5 453.6 all-gather.1
  1435.3 24.9 reduce-scatter.1
where the time goes:
time: 1470 us
  blocking collectives  850 us (58%)
  waiting for transfers between devices  470 us (32%)
  local copies, waits for them, and re-layouts  95.6 us (7%)
  matrix products  34.5 us (2%)
    all_to_all x1, blocking collectives, per_device(): lax.all_to_all(outgoing, 'row', split_axis=2, concat_axis=2, tiled=True)  850 us
    all_gather x1, waiting for transfers between devices, per_device(): gathered = lax.all_gather(factors, 'row', axis=0, tiled=True)  445 us
    reshape x1, local copies, waits for them, and re-layouts, block_terms(): products.astype(jnp.bfloat16)  65 us
  transfers between devices with their start and end apart: 2, of which 2 were waited for; matrix products, arithmetic and copies ran while one was open for 1% of the time, Pallas kernels for 0%

commit v1 on v0

v1 whole, which is shorter than its diff:
```python
import jax
import jax.numpy as jnp
from jax import lax
from jax.experimental import pallas as pl
from jax.experimental.pallas import tpu as pltpu
from jax.sharding import PartitionSpec as P

LANES = 128
SUB = 16
GROUP = 8


def ladder_kernel(mix_ref, block_ref, out_ref, mixed):
    slab = block_ref.shape[1]
    vir = block_ref.shape[2]
    step = pl.program_id(0)

    @pl.when(step == 0)
    def _():
        out_ref[...] = jnp.zeros_like(out_ref)

    def mix(at, carry):
        first = pl.multiple_of(at * (SUB * GROUP), SUB * GROUP)
        wide = jnp.concatenate(
            [
                block_ref[0, :, pl.ds(first + j * SUB, SUB), :].reshape(slab * SUB, LANES)
                for j in range(GROUP)
            ],
            axis=1,
        )
        result = jnp.dot(mix_ref[...], wide, preferred_element_type=jnp.float32).astype(jnp.bfloat16)
        for j in range(GROUP):
            for c in range(slab):
                mixed[pl.ds(first + j * SUB, SUB), c * LANES : (c + 1) * LANES] = result[
                    c * SUB : (c + 1) * SUB, j * LANES : (j + 1) * LANES
                ]
        return carry

    lax.fori_loop(0, vir // (SUB * GROUP), mix, 0)

    tile = 256

    def multiply(at, carry):
        first = pl.multiple_of(at * tile, tile)
        left = jnp.concatenate([block_ref[0, c, pl.ds(first, tile), :] for c in range(slab)], axis=1)
        out_ref[pl.ds(first, tile), :] += lax.dot_general(
            left, mixed[...], (((1,), (1,)), ((), ())), preferred_element_type=jnp.float32
        )
        return carry

    lax.fori_loop(0, vir // tile, multiply, 0)


def ladder(blocks, amplitudes):
    count, slab, vir, _ = blocks.shape
    mix = jnp.kron(amplitudes, jnp.eye(SUB, dtype=amplitudes.dtype))
    return pl.pallas_call(
        ladder_kernel,
        grid=(count,),
        in_specs=[
            pl.BlockSpec((slab * SUB, slab * SUB), lambda i: (0, 0)),
            pl.BlockSpec((1, slab, vir, LANES), lambda i: (i, 0, 0, 0)),
        ],
        out_specs=pl.BlockSpec((vir, vir), lambda i: (0, 0)),
        out_shape=jax.ShapeDtypeStruct((vir, vir), jnp.float32),
        scratch_shapes=[pltpu.VMEM((vir, slab * LANES), jnp.bfloat16)],
        compiler_params=pltpu.CompilerParams(vmem_limit_bytes=32 * 1024 * 1024),
        cost_estimate=pl.CostEstimate(
            flops=2 * vir * vir * slab * LANES * count,
            bytes_accessed=2 * count * slab * vir * LANES,
            transcendentals=0,
        ),
    )(mix, blocks)


def per_device(factors, amplitudes, vir_energy, pair_energy):
    row_count, slab, aux = factors.shape
    pairs = amplitudes.shape[0]
    vir = vir_energy.shape[0]
    rows = lax.axis_size("row")
    cols = lax.axis_size("col")
    here_row = lax.axis_index("row")
    here_col = lax.axis_index("col")
    share = pairs // cols
    piece = aux // rows
    depth = piece * cols

    outgoing = factors.reshape(row_count, slab, rows, piece).transpose(2, 1, 0, 3)
    swapped = lax.all_to_all(outgoing, "row", split_axis=0, concat_axis=0, tiled=True)
    gathered = lax.all_gather(swapped, "col", axis=0, tiled=False)
    whole = gathered.transpose(2, 1, 3, 0, 4).reshape(slab, vir, depth)
    mine = lax.dynamic_slice_in_dim(amplitudes, here_col * share, share, 0)
    if depth % LANES == 0 and vir % 256 == 0:
        blocks = whole.reshape(slab, vir, depth // LANES, LANES).transpose(2, 0, 1, 3)
        partial = jnp.stack([ladder(blocks, mine[p]) for p in range(share)])
    else:
        mixed = jnp.einsum(
            "pcd,dbq->pcbq", mine, whole, preferred_element_type=jnp.float32
        ).astype(jnp.bfloat16)
        partial = jnp.einsum("caq,pcbq->pab", whole, mixed, preferred_element_type=jnp.float32)
    reduced = lax.psum_scatter(partial, "row", scatter_dimension=1, tiled=True)
    first_energy = lax.dynamic_slice_in_dim(vir_energy, here_row * row_count, row_count)
    pair_here = lax.dynamic_slice_in_dim(pair_energy, here_col * share, share)
    divisor = first_energy[None, :, None] + vir_energy[None, None, :] - pair_here[:, None, None]
    return (reduced, reduced / divisor)


def solution(mesh):
    return jax.shard_map(
        per_device,
        mesh=mesh,
        in_specs=(P("row", None, "col"), P(), P(), P()),
        out_specs=(P("col", "row", None), P("col", "row", None)),
        check_vma=False,
    )
```

time: 1470 us -> 374 us (0.25)
  blocking collectives: 850 us -> 94.7 us
  waiting for transfers between devices: 470 us -> 167 us
  matrix products: 34.5 us -> 0 us
  local copies, waits for them, and re-layouts: 95.6 us -> 71.7 us
  Pallas kernels: 0 us -> 22.4 us
    all_to_all x1, blocking collectives: 850 us -> 94.7 us  [per_device(): lax.all_to_all(outgoing, 'row', split_axis=0, concat_axis=0, tiled=True)]
    all_gather x1, waiting for transfers between devices: 445 us -> 98.2 us  [per_device(): gathered = lax.all_gather(swapped, 'col', axis=0, tiled=False)]
    reshape x4 -> x0, local copies, waits for them, and re-layouts: 76.1 us -> none  [the longest x1 65 us: block_terms(): products.astype(jnp.bfloat16)]
    reduce_scatter x1, waiting for transfers between devices: 24.4 us -> 68.4 us  [per_device(): reduced = lax.psum_scatter(partial, 'row', scatter_dimension=1, tiled=True)]
    another operation x1 -> x2, local copies, waits for them, and re-layouts: 0.12 us -> 41 us  [per_device(): whole.reshape(slab, vir, depth // LANES, LANES).transpose(2, 0, 1, 3)]
    dot_general x3 -> x0, matrix products: 34.5 us -> none  [the longest x1 14 us: mirror_term(): jnp.einsum('bdac,pcd->pab', products, amplitudes, preferred_element_type=...]
    pallas_call x0 -> x1, Pallas kernels: none -> 22.4 us  [ladder(): pl.pallas_call(ladder_kernel, grid=(count,), in_specs=[pl.BlockSpec((slab...]
    all_gather x0 -> x1, local copies, waits for them, and re-layouts: none -> 16.7 us  [per_device(): gathered = lax.all_gather(swapped, 'col', axis=0, tiled=False)]
  transfers between devices with their start and end apart: 2 -> 2, of which waited for: 2 -> 2; matrix products, arithmetic and copies ran while one was open for 1% -> 0% of each run, Pallas kernels for 0% -> 0%
where the time goes in v1:
time: 374 us; the launch traced here: 372 us
  waiting for transfers between devices  167 us (45%)
  blocking collectives  94.7 us (25%)
  local copies, waits for them, and re-layouts  71.7 us (19%)
  Pallas kernels  22.4 us (6%)
  between operations  14.1 us (4%)
    all_gather x1, waiting for transfers between devices, per_device(): gathered = lax.all_gather(swapped, 'col', axis=0, tiled=False)  98.2 us
    all_to_all x1, blocking collectives, per_device(): lax.all_to_all(outgoing, 'row', split_axis=0, concat_axis=0, tiled=True)  94.7 us
    reduce_scatter x1, waiting for transfers between devices, per_device(): reduced = lax.psum_scatter(partial, 'row', scatter_dimension=1, tiled=True)  68.4 us
    another operation x2, local copies, waits for them, and re-layouts, per_device(): whole.reshape(slab, vir, depth // LANES, LANES).transpose(2, 0, 1, 3)  41 us
    pallas_call x1, Pallas kernels, ladder(): pl.pallas_call(ladder_kernel, grid=(count,), in_specs=[pl.BlockSpec((slab...  22.4 us
    all_gather x1, local copies, waits for them, and re-layouts, per_device(): gathered = lax.all_gather(swapped, 'col', axis=0, tiled=False)  16.7 us
    unnamed x12, local copies, waits for them, and re-layouts  10.1 us
  transfers between devices with their start and end apart: 2, of which 2 were waited for; matrix products, arithmetic and copies ran while one was open for 0% of the time, Pallas kernels for 0%

profile of v1, /device:TPU:0, one launch (start us, length us, event | category | flops | bytes accessed | tf_op | source)
XLA Modules:
  0.0 372.4 jit_solution(3964739431878890330)
XLA Ops:
  7.2 0.0 copy-start
  7.2 0.0 all-gather.3.cloned.1.call-start
  7.2 5.7 %copy.16 = bf16[96,12,1280]{0,2,1:T(8,128)(2,1)} copy(bf16[96,12,1280]{2,0,1:T(8,128)(2,1)} %param.4) | data formatting | bytes 5898240 | tf_op args[0]
  12.9 2.5 copy.17
  15.4 94.7 %all_to_all.5 = bf16[8,12,96,160]{2,3,1,0:T(8,128)(2,1)} all-to-all(bf16[8,12,96,160]{2,3,1,0:T(8,128)(2,1)S(1)} %copy.17), channel_id=1, replica_groups=mesh['row'=8,'col'=4] {'row'}, dimensions={0} | all-to-all | bytes 5898240 | tf_op jit(solution)/shard_map/all_to_all | solution.py:89
  110.2 0.0 all-gather.3.cloned.1.call-update
  110.2 0.0 reduce-scatter.2.cloned.1.call-start
  110.3 0.0 copy-done
  110.3 0.1 broadcast_multiply_fusion
  110.4 0.7 mul.33.mix_ref
  111.1 98.2 %all-gather.3.cloned.1.call-done = bf16[32,12,96,160]{2,3,1,0:T(8,128)(2,1)} async-done(((bf16[8,12,96,160]{2,3,1,0:T(8,128)(2,1)}), bf16[32,12,96,160]{2,3,1,0:T(8,128)(2,1)}) %all-gather.3.cloned.1.call-update) | async-done | bytes 11796496 | tf_op jit(solution)/shard_map/all_gather | solution.py:90
  209.3 16.7 %copy.23 = bf16[4,8,12,96,160]{3,1,4,0,2:T(8,128)(2,1)} copy(bf16[4,8,12,96,160]{3,4,2,1,0:T(8,128)(2,1)} %bitcast.19) | data formatting | bytes 23592960 | tf_op jit(solution)/shard_map/all_gather | solution.py:90
  226.1 24.7 %reshape_reshape.3 = bf16[12,768,5,128]{1,3,2,0:T(8,128)(2,1)} reshape(bf16[12,8,96,4,160]{2,1,4,3,0:T(8,128)(2,1)} %bitcast.18) | data formatting | bytes 23592960 | tf_op jit(solution)/shard_map/reshape;reshape | solution.py:94
  250.8 16.3 %copy.19 = bf16[12,768,5,128]{3,1,0,2:T(8,128)(2,1)} copy(bf16[12,768,5,128]{1,3,2,0:T(8,128)(2,1)} %reshape_reshape.3) | data formatting | bytes 23592960 | tf_op jit(solution)/shard_map/reshape;reshape | solution.py:94
  267.1 0.0 copy-start.2
  267.1 4.3 %copy-done.2 = bf16[12,768,5,128]{3,1,0,2:T(8,128)(2,1)S(1)} copy-done((bf16[12,768,5,128]{3,1,0,2:T(8,128)(2,1)S(1)}, bf16[12,768,5,128]{3,1,0,2:T(8,128)(2,1)}, u32[]{:S(2)}) %copy-start.2) | copy-done | bytes 11796504
  271.4 0.0 copy-start.4
  271.4 0.0 copy-start.3
  271.4 0.0 copy-start.1
  271.5 22.4 %shard_map.59 = f32[768,768]{1,0:T(8,128)} custom-call(bf16[192,192]{1,0:T(8,128)(2,1)S(1)} %mul.33.mix_ref, bf16[5,12,768,128]{3,2,1,0:T(8,128)(2,1)S(1)} %bitcast.17), custom_call_target="tpu_custom_call" | custom-call | flops 9059696640 | bytes 11796480 | tf_op jit(solution)/shard_map/pallas_call | solution.py:57
  293.9 0.0 reduce-scatter.2.cloned.1.call-update
  293.9 0.0 copy-done.4
  293.9 0.7 dynamic_slice.11
  294.6 0.0 copy-done.3
  294.6 0.1 dynamic_slice.10
  294.7 68.4 %reduce-scatter.2.cloned.1.call-done = f32[1,96,768]{2,1,0:T(8,128)} async-done(((f32[1,768,768]{2,1,0:T(8,128)}), f32[1,96,768]{2,1,0:T(8,128)}) %reduce-scatter.2.cloned.1.call-update) | async-done | bytes 294928 | tf_op jit(solution)/shard_map/reduce_scatter | solution.py:101
  363.1 2.5 subtract_divide_fusion
  365.6 0.0 copy-done.1
  (3 shorter events, 0.0 us)
Async XLA Ops:
  7.2 103.1 %copy-start = (bf16[4,12,12]{2,0,1:T(4,128)(2,1)S(1)}, bf16[4,12,12]{2,0,1:T(4,128)(2,1)}, u32[]{:S(2)}) copy-start(bf16[4,12,12]{2,0,1:T(4,128)(2,1)} %param.5) | copy-start | bytes 3460
  7.2 202.2 %all-gather.3.cloned.1.call-start = ((), (), s32[]{:S(2)}) async-start(), calls=%async_computation.3 | async-start | bytes 19660800 | tf_op jit(solution)/shard_map/all_gather | solution.py:90
  110.2 252.9 %reduce-scatter.2.cloned.1.call-start = ((), (), s32[]{:S(2)}) async-start(), calls=%async_computation.2 | async-start | bytes 2654208 | tf_op jit(solution)/shard_map/reduce_scatter | solution.py:101
  267.1 4.4 %copy-start.2 = (bf16[12,768,5,128]{3,1,0,2:T(8,128)(2,1)S(1)}, bf16[12,768,5,128]{3,1,0,2:T(8,128)(2,1)}, u32[]{:S(2)}) copy-start(bf16[12,768,5,128]{3,1,0,2:T(8,128)(2,1)} %copy.19) | copy-start | bytes 35389444
  271.4 22.5 %copy-start.4 = (f32[4]{0:T(128)S(1)}, f32[4]{0:T(128)}, u32[]{:S(2)}) copy-start(f32[4]{0:T(128)} %param.7) | copy-start | bytes 52
  271.4 23.2 %copy-start.3 = (f32[768]{0:T(1024)S(1)}, f32[768]{0:T(1024)}, u32[]{:S(2)}) copy-start(f32[768]{0:T(1024)} %param.6) | copy-start | bytes 9220
  271.4 94.1 %copy-start.1 = (bf16[4,12,12]{2,0,1:T(4,128)(2,1)S(1)}, bf16[4,12,12]{2,0,1:T(4,128)(2,1)}, u32[]{:S(2)}) copy-start(bf16[4,12,12]{2,0,1:T(4,128)(2,1)} %param.5) | copy-start | bytes 3460
Sparse Core Ops, SparseCore 0:
  110.3 98.9 all-gather.2
  294.0 68.9 reduce-scatter.1

commit v2 on v1

--- a/solution.py
+++ b/solution.py
@@ -73,6 +73,325 @@
     )(mix, blocks)
 
 
+def flip(index, bits):
+    low, mid, high = index % 2, (index // 2) % 2, index // 4
+    b0, b1, b2 = bits % 2, (bits // 2) % 2, bits // 4
+    return (low + b0) % 2 + 2 * ((mid + b1) % 2) + 4 * ((high + b2) % 2)
+
+
+def visit_order(step):
+    return step % 2 + 4 * ((step // 2) % 2) + 2 * (step // 4)
+
+
+def fused_kernel(
+    mix_ref,
+    blocks_ref,
+    first_ref,
+    second_ref,
+    pair_ref,
+    residual_ref,
+    update_ref,
+    held,
+    mixed,
+    partial,
+    y_in,
+    z_in,
+    local_sem,
+    row_send,
+    extra_send,
+    side_send,
+    cross_send,
+    arrive,
+    y_send,
+    y_arrive,
+    z_send,
+    z_arrive,
+):
+    row = lax.axis_index("row")
+    col = lax.axis_index("col")
+    slab, rows, row_count = held.shape[1], held.shape[2], held.shape[3]
+    side = flip(col, 1)
+    cross = flip(col, 2)
+    corner = flip(col, 3)
+    owner = row % 4
+
+    def at(row_id, col_id):
+        return (row_id, col_id)
+
+    barrier = pltpu.get_barrier_semaphore()
+    peers = [at(flip(row, j), col) for j in range(1, rows)] + [at(row, side), at(row, cross)]
+    for peer in peers:
+        pl.semaphore_signal(barrier, inc=1, device_id=peer, device_id_type=pl.DeviceIdType.MESH)
+    pl.semaphore_wait(barrier, len(peers))
+
+    def remote(src, dst, send, recv, device):
+        return pltpu.make_async_remote_copy(
+            src_ref=src,
+            dst_ref=dst,
+            send_sem=send,
+            recv_sem=recv,
+            device_id=device,
+            device_id_type=pl.DeviceIdType.MESH,
+        )
+
+    def row_copy(j):
+        other = flip(row, j)
+        return remote(
+            blocks_ref.at[other], held.at[col, :, row], row_send.at[j], arrive.at[col, row], at(other, col)
+        )
+
+    def extra_copy(e):
+        return remote(
+            blocks_ref.at[rows + e], held.at[4, :, row], extra_send.at[e], arrive.at[4, row], at(col + 4 * e, col)
+        )
+
+    def forward(slot, source, device, send):
+        return remote(held.at[slot, :, source], held.at[slot, :, source], send, arrive.at[slot, source], device)
+
+    def landed(slot, source):
+        forward(slot, source, at(row, side), side_send.at[slot, source]).wait_recv()
+
+    own = pltpu.make_async_copy(blocks_ref.at[row], held.at[col, :, row], local_sem.at[0])
+    own.start()
+    for step in range(1, rows):
+        row_copy(visit_order(step)).start()
+        if step in (2, 3):
+            e = step - 2
+
+            @pl.when(row != col + 4 * e)
+            def _():
+                extra_copy(e).start()
+
+    @pl.when(owner == col)
+    def _():
+        own_extra = pltpu.make_async_copy(blocks_ref.at[rows + row // 4], held.at[4, :, row], local_sem.at[1])
+        own_extra.start()
+        own_extra.wait()
+
+    own.wait()
+
+    def mix(slot, source):
+        groups = row_count // SUB
+        wide = jnp.concatenate(
+            [
+                held[slot, :, source, j * SUB : (j + 1) * SUB, :].reshape(slab * SUB, LANES)
+                for j in range(groups)
+            ],
+            axis=1,
+        )
+        result = jnp.dot(mix_ref[...], wide, preferred_element_type=jnp.float32).astype(jnp.bfloat16)
+        for j in range(groups):
+            for c in range(slab):
+                mixed[slot, source, j * SUB : (j + 1) * SUB, c * LANES : (c + 1) * LANES] = result[
+                    c * SUB : (c + 1) * SUB, j * LANES : (j + 1) * LANES
+                ]
+
+    def gather_step(step, carry):
+        @pl.when(step < rows)
+        def _():
+            source = flip(row, visit_order(step))
+
+            @pl.when(step > 0)
+            def _():
+                landed(col, source)
+
+            forward(col, source, at(row, cross), cross_send.at[0, source]).start()
+            forward(col, source, at(row, side), side_send.at[col, source]).start()
+
+            @pl.when(owner == col)
+            def _():
+                @pl.when(step > 0)
+                def _():
+                    landed(4, source)
+
+                forward(4, source, at(row, cross), cross_send.at[1, source]).start()
+                forward(4, source, at(row, side), side_send.at[4, source]).start()
+
+        @pl.when((step >= 1) & (step < rows + 1))
+        def _():
+            source = flip(row, visit_order(step - 1))
+            landed(cross, source)
+            forward(cross, source, at(row, side), side_send.at[cross, source]).start()
+
+            @pl.when(owner == cross)
+            def _():
+                landed(4, source)
+                forward(4, source, at(row, side), side_send.at[4, source]).start()
+
+        @pl.when(step >= 2)
+        def _():
+            source = flip(row, visit_order(step - 2))
+            landed(side, source)
+            landed(corner, source)
+
+            @pl.when((owner == side) | (owner == corner))
+            def _():
+                landed(4, source)
+
+            def mix_slot(slot, inner):
+                mix(slot, source)
+                return inner
+
+            lax.fori_loop(0, 5, mix_slot, 0)
+
+        return carry
+
+    lax.fori_loop(0, rows + 2, gather_step, 0)
+
+    y_here, z_here = row % 2, row // 2
+    y_peer = flip(row, 1)
+
+    def tile_of(step):
+        high = 1 - step // 2
+        low = (step % 2 + step // 2) % 2
+        return flip(z_here, 2 * high + low)
+
+    def y_copy(tile):
+        return remote(
+            partial.at[tile, 1 - y_here], y_in.at[tile], y_send.at[tile], y_arrive.at[tile], at(y_peer, col)
+        )
+
+    def z_copy(tile):
+        return remote(
+            partial.at[tile, y_here],
+            z_in.at[z_here],
+            z_send.at[tile],
+            z_arrive.at[z_here],
+            at(2 * tile + y_here, col),
+        )
+
+    def z_landed(source):
+        remote(
+            partial.at[source, y_here],
+            z_in.at[source],
+            z_send.at[source],
+            z_arrive.at[source],
+            at(2 * source + y_here, col),
+        ).wait_recv()
+
+    def reduce_step(step, carry):
+        @pl.when(step < 4)
+        def _():
+            tile = tile_of(step)
+
+            def multiply(slot, inner):
+                left = jnp.concatenate(
+                    [held[slot, c, pl.ds(2 * tile, 2)].reshape(2 * row_count, LANES) for c in range(slab)], axis=1
+                )
+                right = mixed[slot].reshape(rows * row_count, slab * LANES)
+                product = lax.dot_general(
+                    left, right, (((1,), (1,)), ((), ())), preferred_element_type=jnp.float32
+                ).reshape(2, row_count, rows * row_count)
+
+                @pl.when(slot == 0)
+                def _():
+                    partial[tile] = product
+
+                @pl.when(slot > 0)
+                def _():
+                    partial[tile] += product
+
+                return inner
+
+            lax.fori_loop(0, 5, multiply, 0)
+            y_copy(tile).start()
+
+        @pl.when(step >= 1)
+        def _():
+            tile = tile_of(step - 1)
+            y_copy(tile).wait_recv()
+            partial[tile, y_here] += y_in[tile]
+
+            @pl.when(step < 4)
+            def _():
+                z_copy(tile).start()
+
+        return carry
+
+    lax.fori_loop(0, 5, reduce_step, 0)
+
+    for j in range(1, 4):
+        source = flip(z_here, j)
+        z_landed(source)
+        partial[z_here, y_here] += z_in[source]
+    total = partial[z_here, y_here]
+    residual_ref[0] = total
+    update_ref[0] = total / (first_ref[...] + second_ref[...] - pair_ref[...])
+
+    for j in range(1, rows):
+        row_copy(j).wait_send()
+    for e in range(2):
+
+        @pl.when(row != col + 4 * e)
+        def _():
+            extra_copy(e).wait_send()
+
+    def finish(source, carry):
+        forward(col, source, at(row, cross), cross_send.at[0, source]).wait_send()
+        forward(col, source, at(row, side), side_send.at[col, source]).wait_send()
+        forward(cross, source, at(row, side), side_send.at[cross, source]).wait_send()
+
+        @pl.when(owner == col)
+        def _():
+            forward(4, source, at(row, cross), cross_send.at[1, source]).wait_send()
+
+        @pl.when((owner == col) | (owner == cross))
+        def _():
+            forward(4, source, at(row, side), side_send.at[4, source]).wait_send()
+
+        return carry
+
+    lax.fori_loop(0, rows, finish, 0)
+    for step in range(4):
+        y_copy(tile_of(step)).wait_send()
+    for step in range(3):
+        z_copy(tile_of(step)).wait_send()
+
+
+def fused(factors, amplitudes, vir_energy, pair_energy):
+    row_count, slab, aux = factors.shape
+    vir = vir_energy.shape[0]
+    rows = vir // row_count
+    here_row = lax.axis_index("row")
+    here_col = lax.axis_index("col")
+    blocks = factors.reshape(row_count, slab, aux // LANES, LANES).transpose(2, 1, 0, 3)
+    mine = lax.dynamic_index_in_dim(amplitudes, here_col, 0, keepdims=False)
+    mix = jnp.kron(mine, jnp.eye(SUB, dtype=mine.dtype))
+    first = lax.dynamic_slice_in_dim(vir_energy, here_row * row_count, row_count)[:, None]
+    pair = lax.dynamic_slice_in_dim(pair_energy, here_col, 1)[:, None]
+    result = jax.ShapeDtypeStruct((1, row_count, vir), jnp.float32)
+    dma = pltpu.SemaphoreType.DMA
+    return pl.pallas_call(
+        fused_kernel,
+        in_specs=[pl.BlockSpec(memory_space=pltpu.VMEM)] * 5,
+        out_specs=[pl.BlockSpec(memory_space=pltpu.VMEM)] * 2,
+        out_shape=[result, result],
+        scratch_shapes=[
+            pltpu.VMEM((5, slab, rows, row_count, LANES), jnp.bfloat16),
+            pltpu.VMEM((5, rows, row_count, slab * LANES), jnp.bfloat16),
+            pltpu.VMEM((rows // 2, 2, row_count, vir), jnp.float32),
+            pltpu.VMEM((rows // 2, row_count, vir), jnp.float32),
+            pltpu.VMEM((rows // 2, row_count, vir), jnp.float32),
+            dma((2,)),
+            dma((rows,)),
+            dma((2,)),
+            dma((5, rows)),
+            dma((2, rows)),
+            dma((5, rows)),
+            dma((rows // 2,)),
+            dma((rows // 2,)),
+            dma((rows // 2,)),
+            dma((rows // 2,)),
+        ],
+        compiler_params=pltpu.CompilerParams(
+            collective_id=0, has_side_effects=True, vmem_limit_bytes=52 * 1024 * 1024
+        ),
+        cost_estimate=pl.CostEstimate(
+            flops=2 * vir * vir * slab * LANES * 5, bytes_accessed=4 * factors.size, transcendentals=0
+        ),
+    )(mix, blocks, first, vir_energy[None, :], pair)
+
+
 def per_device(factors, amplitudes, vir_energy, pair_energy):
     row_count, slab, aux = factors.shape
     pairs = amplitudes.shape[0]
@@ -82,6 +401,8 @@
     here_row = lax.axis_index("row")
     here_col = lax.axis_index("col")
     share = pairs // cols
+    if rows == 8 and cols == 4 and share == 1 and aux == 10 * LANES and row_count % SUB == 0:
+        return tuple(fused(factors, amplitudes, vir_energy, pair_energy))
     piece = aux // rows
     depth = piece * cols
 

time: 374 us -> 156 us (0.42)
  the two profiles are of different devices: /device:TPU:0 before, /device:TPU:14 now
where the time goes in v2:
time: 156 us
  Pallas kernels  140 us (90%)
  local copies, waits for them, and re-layouts  15.1 us (10%)
    pallas_call x1, Pallas kernels, fused(): pl.pallas_call(fused_kernel, in_specs=[pl.BlockSpec(memory_space=pltpu.VM...  140 us
    unnamed x10, local copies, waits for them, and re-layouts  7.85 us
    reshape x1, local copies, waits for them, and re-layouts, fused(): factors.reshape(row_count, slab, aux // LANES, LANES).transpose(2, 1, 0, 3)  5.78 us

profile of v2, /device:TPU:14, one launch (start us, length us, event | category | flops | bytes accessed | tf_op | source)
XLA Modules:
  0.0 155.6 jit_solution(16973906280997817919)
XLA Ops:
  0.6 0.0 copy-start
  0.7 0.7 copy-done
  1.4 0.1 broadcast_multiply_fusion
  1.5 0.7 mul.33.mix_ref
  2.2 5.7 %copy.8 = bf16[96,12,1280]{0,2,1:T(8,128)(2,1)} copy(bf16[96,12,1280]{2,0,1:T(8,128)(2,1)} %param.4) | data formatting | bytes 5898240 | tf_op args[0]
  7.9 0.0 copy-start.1
  7.9 0.0 copy-start.2
  7.9 5.8 %copy.9 = bf16[96,12,10,128]{3,0,1,2:T(8,128)(2,1)} copy(bf16[96,12,10,128]{0,3,2,1:T(8,128)(2,1)} %bitcast.8) | data formatting | bytes 5898240 | tf_op jit(solution)/shard_map/reshape | solution.py:357
  13.7 0.0 copy-done.1
  13.7 0.1 dynamic-slice_bitcast_fusion
  13.7 0.1 copy.10.first_ref
  13.9 0.0 copy-done.2
  13.9 0.6 dynamic_slice.12
  14.5 139.7 %shard_map.59 = (f32[1,96,768]{2,1,0:T(8,128)S(1)}, f32[1,96,768]{2,1,0:T(8,128)S(1)}) custom-call(bf16[192,192]{1,0:T(8,128)(2,1)S(1)} %mul.33.mix_ref, bf16[10,12,96,128]{3,2,1,0:T(8,128)(2,1)} %bitcast.9, f32[96,1]{1,0:T(8,128)S(1)} %copy.10.first_ref, f32[1,768]{1,0:T(1,128)S(1)} %broadcast_in_dim.14.second_ref, f32[1,1]{1,0:T(1,128)} %bitcast.4.pair_ref), custom_call_target="tpu_custom_call" | custom-call | flops 9059696640 | bytes 5898240 | tf_op jit(solution)/shard_map/pallas_call | solution.py:364
  154.2 0.7 copy.16
  154.9 0.7 copy.17
  (4 shorter events, 0.0 us)
Async XLA Ops:
  0.6 0.7 copy-start
  7.9 5.8 %copy-start.1 = (f32[768]{0:T(1024)S(1)}, f32[768]{0:T(1024)}, u32[]{:S(2)}) copy-start(f32[768]{0:T(1024)} %param.6) | copy-start | bytes 9220
  7.9 6.0 %copy-start.2 = (f32[4]{0:T(128)S(1)}, f32[4]{0:T(128)}, u32[]{:S(2)}) copy-start(f32[4]{0:T(128)} %param.7) | copy-start | bytes 52

commit v3 on v2

--- a/solution.py
+++ b/solution.py
@@ -79,24 +79,23 @@
     return (low + b0) % 2 + 2 * ((mid + b1) % 2) + 4 * ((high + b2) % 2)
 
 
-def visit_order(step):
-    return step % 2 + 4 * ((step // 2) % 2) + 2 * (step // 4)
-
-
 def fused_kernel(
     mix_ref,
-    blocks_ref,
+    factors_ref,
     first_ref,
     second_ref,
     pair_ref,
     residual_ref,
     update_ref,
+    blocks,
+    packed,
+    halves,
     held,
     mixed,
     partial,
     y_in,
-    z_in,
-    local_sem,
+    near_in,
+    far_in,
     row_send,
     extra_send,
     side_send,
@@ -104,8 +103,10 @@
     arrive,
     y_send,
     y_arrive,
-    z_send,
-    z_arrive,
+    near_send,
+    near_arrive,
+    far_send,
+    far_arrive,
 ):
     row = lax.axis_index("row")
     col = lax.axis_index("col")
@@ -113,7 +114,14 @@
     side = flip(col, 1)
     cross = flip(col, 2)
     corner = flip(col, 3)
-    owner = row % 4
+    core, x_here = col % 2, col // 2
+    y_here, z_here = row % 2, row // 2
+    owner = core == y_here
+    half_rows = row_count // 2
+    low_lane = lax.broadcasted_iota(jnp.int32, (half_rows, LANES), 1) < LANES // 2
+
+    def swap(value):
+        return pltpu.roll(value, LANES // 2, 1)
 
     def at(row_id, col_id):
         return (row_id, col_id)
@@ -122,6 +130,25 @@
     peers = [at(flip(row, j), col) for j in range(1, rows)] + [at(row, side), at(row, cross)]
     for peer in peers:
         pl.semaphore_signal(barrier, inc=1, device_id=peer, device_id_type=pl.DeviceIdType.MESH)
+
+    for b in range(rows):
+        blocks[b] = factors_ref[:, :, b * LANES : (b + 1) * LANES]
+    for t in range(4):
+        start = (rows + t // 2) * LANES
+        for c in range(slab):
+            block = factors_ref[c, :, start : start + LANES].astype(jnp.float32)
+            top, bottom = block[:half_rows], block[half_rows:]
+            if t % 2 == 0:
+                both = jnp.where(low_lane, top, swap(bottom))
+            else:
+                both = jnp.where(low_lane, swap(top), bottom)
+            packed[t, c] = both.astype(jnp.bfloat16)
+    held[col, :, row] = blocks[row]
+
+    @pl.when(owner)
+    def _():
+        halves[x_here, row] = packed[z_here]
+
     pl.semaphore_wait(barrier, len(peers))
 
     def remote(src, dst, send, recv, device):
@@ -137,38 +164,41 @@
     def row_copy(j):
         other = flip(row, j)
         return remote(
-            blocks_ref.at[other], held.at[col, :, row], row_send.at[j], arrive.at[col, row], at(other, col)
-        )
-
-    def extra_copy(e):
+            blocks.at[other], held.at[col, :, row], row_send.at[j], arrive.at[col, row], at(other, col)
+        )
+
+    def extra_copy(d):
+        target = flip(z_here, d)
         return remote(
-            blocks_ref.at[rows + e], held.at[4, :, row], extra_send.at[e], arrive.at[4, row], at(col + 4 * e, col)
+            packed.at[target],
+            halves.at[x_here, row],
+            extra_send.at[d],
+            arrive.at[4 + x_here, row],
+            at(2 * target + core, col),
         )
 
     def forward(slot, source, device, send):
         return remote(held.at[slot, :, source], held.at[slot, :, source], send, arrive.at[slot, source], device)
 
+    def forward_half(x, source, device, send):
+        return remote(halves.at[x, source], halves.at[x, source], send, arrive.at[4 + x, source], device)
+
     def landed(slot, source):
         forward(slot, source, at(row, side), side_send.at[slot, source]).wait_recv()
 
-    own = pltpu.make_async_copy(blocks_ref.at[row], held.at[col, :, row], local_sem.at[0])
-    own.start()
-    for step in range(1, rows):
-        row_copy(visit_order(step)).start()
-        if step in (2, 3):
-            e = step - 2
-
-            @pl.when(row != col + 4 * e)
-            def _():
-                extra_copy(e).start()
-
-    @pl.when(owner == col)
+    def landed_half(x, source):
+        forward_half(x, source, at(row, side), side_send.at[4 + x, source]).wait_recv()
+
+    for j in (4, 1, 2, 3):
+        row_copy(j).start()
+
+    @pl.when(jnp.logical_not(owner))
     def _():
-        own_extra = pltpu.make_async_copy(blocks_ref.at[rows + row // 4], held.at[4, :, row], local_sem.at[1])
-        own_extra.start()
-        own_extra.wait()
-
-    own.wait()
+        extra_copy(0).start()
+
+    extra_copy(1).start()
+    row_copy(5).start()
+    extra_copy(2).start()
 
     def mix(slot, source):
         groups = row_count // SUB
@@ -186,10 +216,19 @@
                     c * SUB : (c + 1) * SUB, j * LANES : (j + 1) * LANES
                 ]
 
+    def unpack(source):
+        for c in range(slab):
+            first = halves[0, source, c].astype(jnp.float32)
+            second = halves[1, source, c].astype(jnp.float32)
+            top = jnp.where(low_lane, first, swap(second))
+            bottom = jnp.where(low_lane, swap(first), second)
+            held[4, c, source, :half_rows] = top.astype(jnp.bfloat16)
+            held[4, c, source, half_rows:] = bottom.astype(jnp.bfloat16)
+
     def gather_step(step, carry):
         @pl.when(step < rows)
         def _():
-            source = flip(row, visit_order(step))
+            source = flip(row, step)
 
             @pl.when(step > 0)
             def _():
@@ -198,35 +237,49 @@
             forward(col, source, at(row, cross), cross_send.at[0, source]).start()
             forward(col, source, at(row, side), side_send.at[col, source]).start()
 
-            @pl.when(owner == col)
+            @pl.when(owner)
             def _():
                 @pl.when(step > 0)
                 def _():
-                    landed(4, source)
-
-                forward(4, source, at(row, cross), cross_send.at[1, source]).start()
-                forward(4, source, at(row, side), side_send.at[4, source]).start()
+                    landed_half(x_here, source)
+
+                forward_half(x_here, source, at(row, cross), cross_send.at[1, source]).start()
+                forward_half(x_here, source, at(row, side), side_send.at[4 + x_here, source]).start()
+
+        @pl.when(step == 4)
+        def _():
+            row_copy(4).wait_send()
+            row_copy(6).start()
+            extra_copy(3).start()
+
+        @pl.when(step == 5)
+        def _():
+            row_copy(5).wait_send()
+            row_copy(7).start()
 
         @pl.when((step >= 1) & (step < rows + 1))
         def _():
-            source = flip(row, visit_order(step - 1))
+            source = flip(row, step - 1)
             landed(cross, source)
             forward(cross, source, at(row, side), side_send.at[cross, source]).start()
 
-            @pl.when(owner == cross)
-            def _():
-                landed(4, source)
-                forward(4, source, at(row, side), side_send.at[4, source]).start()
+            @pl.when(owner)
+            def _():
+                landed_half(1 - x_here, source)
+                forward_half(1 - x_here, source, at(row, side), side_send.at[5 - x_here, source]).start()
 
         @pl.when(step >= 2)
         def _():
-            source = flip(row, visit_order(step - 2))
+            source = flip(row, step - 2)
             landed(side, source)
             landed(corner, source)
 
-            @pl.when((owner == side) | (owner == corner))
-            def _():
-                landed(4, source)
+            @pl.when(jnp.logical_not(owner))
+            def _():
+                landed_half(0, source)
+                landed_half(1, source)
+
+            unpack(source)
 
             def mix_slot(slot, inner):
                 mix(slot, source)
@@ -238,36 +291,31 @@
 
     lax.fori_loop(0, rows + 2, gather_step, 0)
 
-    y_here, z_here = row % 2, row // 2
     y_peer = flip(row, 1)
 
     def tile_of(step):
-        high = 1 - step // 2
-        low = (step % 2 + step // 2) % 2
-        return flip(z_here, 2 * high + low)
+        return flip(z_here, 3 - step)
 
     def y_copy(tile):
         return remote(
             partial.at[tile, 1 - y_here], y_in.at[tile], y_send.at[tile], y_arrive.at[tile], at(y_peer, col)
         )
 
-    def z_copy(tile):
+    def near_copy(stage):
+        tile = flip(z_here, 3 - 2 * stage)
         return remote(
             partial.at[tile, y_here],
-            z_in.at[z_here],
-            z_send.at[tile],
-            z_arrive.at[z_here],
-            at(2 * tile + y_here, col),
-        )
-
-    def z_landed(source):
-        remote(
-            partial.at[source, y_here],
-            z_in.at[source],
-            z_send.at[source],
-            z_arrive.at[source],
-            at(2 * source + y_here, col),
-        ).wait_recv()
+            near_in.at[stage],
+            near_send.at[stage],
+            near_arrive.at[stage],
+            at(flip(row, 2), col),
+        )
+
+    def far_copy():
+        tile = flip(z_here, 2)
+        return remote(
+            partial.at[tile, y_here], far_in, far_send.at[0], far_arrive.at[0], at(flip(row, 4), col)
+        )
 
     def reduce_step(step, carry):
         @pl.when(step < 4)
@@ -302,50 +350,59 @@
             y_copy(tile).wait_recv()
             partial[tile, y_here] += y_in[tile]
 
-            @pl.when(step < 4)
-            def _():
-                z_copy(tile).start()
+            @pl.when(step == 1)
+            def _():
+                near_copy(0).start()
+
+            @pl.when(step == 2)
+            def _():
+                near_copy(0).wait_recv()
+                partial[tile, y_here] += near_in[0]
+                far_copy().start()
+
+            @pl.when(step == 3)
+            def _():
+                near_copy(1).start()
 
         return carry
 
     lax.fori_loop(0, 5, reduce_step, 0)
 
-    for j in range(1, 4):
-        source = flip(z_here, j)
-        z_landed(source)
-        partial[z_here, y_here] += z_in[source]
-    total = partial[z_here, y_here]
+    near_copy(1).wait_recv()
+    far_copy().wait_recv()
+    total = partial[z_here, y_here] + near_in[1] + far_in[...]
     residual_ref[0] = total
     update_ref[0] = total / (first_ref[...] + second_ref[...] - pair_ref[...])
 
-    for j in range(1, rows):
+    for j in (1, 2, 3, 6, 7):
         row_copy(j).wait_send()
-    for e in range(2):
-
-        @pl.when(row != col + 4 * e)
-        def _():
-            extra_copy(e).wait_send()
+
+    @pl.when(jnp.logical_not(owner))
+    def _():
+        extra_copy(0).wait_send()
+
+    for d in range(1, 4):
+        extra_copy(d).wait_send()
 
     def finish(source, carry):
         forward(col, source, at(row, cross), cross_send.at[0, source]).wait_send()
         forward(col, source, at(row, side), side_send.at[col, source]).wait_send()
         forward(cross, source, at(row, side), side_send.at[cross, source]).wait_send()
 
-        @pl.when(owner == col)
-        def _():
-            forward(4, source, at(row, cross), cross_send.at[1, source]).wait_send()
-
-        @pl.when((owner == col) | (owner == cross))
-        def _():
-            forward(4, source, at(row, side), side_send.at[4, source]).wait_send()
+        @pl.when(owner)
+        def _():
+            forward_half(x_here, source, at(row, cross), cross_send.at[1, source]).wait_send()
+            forward_half(x_here, source, at(row, side), side_send.at[4 + x_here, source]).wait_send()
+            forward_half(1 - x_here, source, at(row, side), side_send.at[5 - x_here, source]).wait_send()
 
         return carry
 
     lax.fori_loop(0, rows, finish, 0)
     for step in range(4):
         y_copy(tile_of(step)).wait_send()
-    for step in range(3):
-        z_copy(tile_of(step)).wait_send()
+    near_copy(0).wait_send()
+    near_copy(1).wait_send()
+    far_copy().wait_send()
 
 
 def fused(factors, amplitudes, vir_energy, pair_energy):
@@ -354,7 +411,7 @@
     rows = vir // row_count
     here_row = lax.axis_index("row")
     here_col = lax.axis_index("col")
-    blocks = factors.reshape(row_count, slab, aux // LANES, LANES).transpose(2, 1, 0, 3)
+    slabs = factors.transpose(1, 0, 2)
     mine = lax.dynamic_index_in_dim(amplitudes, here_col, 0, keepdims=False)
     mix = jnp.kron(mine, jnp.eye(SUB, dtype=mine.dtype))
     first = lax.dynamic_slice_in_dim(vir_energy, here_row * row_count, row_count)[:, None]
@@ -367,21 +424,26 @@
         out_specs=[pl.BlockSpec(memory_space=pltpu.VMEM)] * 2,
         out_shape=[result, result],
         scratch_shapes=[
+            pltpu.VMEM((rows, slab, row_count, LANES), jnp.bfloat16),
+            pltpu.VMEM((4, slab, row_count // 2, LANES), jnp.bfloat16),
+            pltpu.VMEM((2, rows, slab, row_count // 2, LANES), jnp.bfloat16),
             pltpu.VMEM((5, slab, rows, row_count, LANES), jnp.bfloat16),
             pltpu.VMEM((5, rows, row_count, slab * LANES), jnp.bfloat16),
             pltpu.VMEM((rows // 2, 2, row_count, vir), jnp.float32),
             pltpu.VMEM((rows // 2, row_count, vir), jnp.float32),
-            pltpu.VMEM((rows // 2, row_count, vir), jnp.float32),
-            dma((2,)),
+            pltpu.VMEM((2, row_count, vir), jnp.float32),
+            pltpu.VMEM((row_count, vir), jnp.float32),
             dma((rows,)),
-            dma((2,)),
-            dma((5, rows)),
+            dma((4,)),
+            dma((6, rows)),
             dma((2, rows)),
-            dma((5, rows)),
+            dma((6, rows)),
             dma((rows // 2,)),
             dma((rows // 2,)),
-            dma((rows // 2,)),
-            dma((rows // 2,)),
+            dma((2,)),
+            dma((2,)),
+            dma((1,)),
+            dma((1,)),
         ],
         compiler_params=pltpu.CompilerParams(
             collective_id=0, has_side_effects=True, vmem_limit_bytes=52 * 1024 * 1024
@@ -389,7 +451,7 @@
         cost_estimate=pl.CostEstimate(
             flops=2 * vir * vir * slab * LANES * 5, bytes_accessed=4 * factors.size, transcendentals=0
         ),
-    )(mix, blocks, first, vir_energy[None, :], pair)
+    )(mix, slabs, first, vir_energy[None, :], pair)
 
 
 def per_device(factors, amplitudes, vir_energy, pair_energy):
@@ -401,7 +463,7 @@
     here_row = lax.axis_index("row")
     here_col = lax.axis_index("col")
     share = pairs // cols
-    if rows == 8 and cols == 4 and share == 1 and aux == 10 * LANES and row_count % SUB == 0:
+    if rows == 8 and cols == 4 and share == 1 and aux == 10 * LANES and row_count % (2 * SUB) == 0:
         return tuple(fused(factors, amplitudes, vir_energy, pair_energy))
     piece = aux // rows
     depth = piece * cols

time: 156 us -> 134 us (0.86)
  the two profiles are of different devices: /device:TPU:14 before, /device:TPU:0 now
where the time goes in v3:
time: 134 us; the launch traced here: 133 us
  Pallas kernels  127 us (95%)
  local copies, waits for them, and re-layouts  5.6 us (4%)
    pallas_call x1, Pallas kernels, fused(): pl.pallas_call(fused_kernel, in_specs=[pl.BlockSpec(memory_space=pltpu.VM...  127 us

profile of v3, /device:TPU:0, one launch (start us, length us, event | category | flops | bytes accessed | tf_op | source)
XLA Modules:
  0.0 133.3 jit_solution(9926144578826614098)
XLA Ops:
  0.6 0.0 copy-start
  0.6 0.7 copy-done
  1.4 0.1 broadcast_multiply_fusion
  1.5 0.7 mul.33.mix_ref
  2.2 1.2 dynamic_slice.12
  3.4 0.8 dynamic-slice_bitcast_fusion
  4.2 0.1 copy.8.first_ref
  4.3 0.7 broadcast_in_dim.14.second_ref
  5.0 126.9 %shard_map.59 = (f32[1,96,768]{2,1,0:T(8,128)S(1)}, f32[1,96,768]{2,1,0:T(8,128)S(1)}) custom-call(bf16[192,192]{1,0:T(8,128)(2,1)S(1)} %mul.33.mix_ref, bf16[12,96,1280]{2,1,0:T(8,128)(2,1)} %bitcast.8, f32[96,1]{1,0:T(8,128)S(1)} %copy.8.first_ref, f32[1,768]{1,0:T(1,128)S(1)} %broadcast_in_dim.14.second_ref, f32[1,1]{1,0:T(1,128)} %bitcast.3.pair_ref), custom_call_target="tpu_custom_call" | custom-call | flops 9059696640 | bytes 5898240 | tf_op jit(solution)/shard_map/pallas_call | solution.py:421
  131.8 0.7 copy.14
  132.5 0.7 copy.15
  (3 shorter events, 0.0 us)
Async XLA Ops:
  0.6 0.7 copy-start

commit v4 on v3

--- a/solution.py
+++ b/solution.py
@@ -80,10 +80,9 @@
 
 
 def fused_kernel(
-    mix_ref,
+    amplitude_ref,
     factors_ref,
-    first_ref,
-    second_ref,
+    energy_ref,
     pair_ref,
     residual_ref,
     update_ref,
@@ -92,6 +91,7 @@
     halves,
     held,
     mixed,
+    mix_matrix,
     partial,
     y_in,
     near_in,
@@ -131,8 +131,63 @@
     for peer in peers:
         pl.semaphore_signal(barrier, inc=1, device_id=peer, device_id_type=pl.DeviceIdType.MESH)
 
-    for b in range(rows):
-        blocks[b] = factors_ref[:, :, b * LANES : (b + 1) * LANES]
+    def cut(index):
+        return factors_ref[:, :, pl.ds(pl.multiple_of(index * LANES, LANES), LANES)]
+
+    def cut_for(j):
+        other = flip(row, j)
+        blocks[other] = cut(other)
+
+    cut_for(4)
+    cut_for(1)
+    pl.semaphore_wait(barrier, len(peers))
+
+    def remote(src, dst, send, recv, device):
+        return pltpu.make_async_remote_copy(
+            src_ref=src,
+            dst_ref=dst,
+            send_sem=send,
+            recv_sem=recv,
+            device_id=device,
+            device_id_type=pl.DeviceIdType.MESH,
+        )
+
+    def row_copy(j):
+        other = flip(row, j)
+        return remote(
+            blocks.at[other], held.at[col, :, row], row_send.at[j], arrive.at[col, row], at(other, col)
+        )
+
+    def extra_copy(d):
+        target = flip(z_here, d)
+        return remote(
+            packed.at[target],
+            halves.at[x_here, row],
+            extra_send.at[d],
+            arrive.at[4 + x_here, row],
+            at(2 * target + core, col),
+        )
+
+    def forward(slot, source, device, send):
+        return remote(held.at[slot, :, source], held.at[slot, :, source], send, arrive.at[slot, source], device)
+
+    def forward_half(x, source, device, send):
+        return remote(halves.at[x, source], halves.at[x, source], send, arrive.at[4 + x, source], device)
+
+    def landed(slot, source):
+        forward(slot, source, at(row, side), side_send.at[slot, source]).wait_recv()
+
+    def landed_half(x, source):
+        forward_half(x, source, at(row, side), side_send.at[4 + x, source]).wait_recv()
+
+    row_copy(4).start()
+    row_copy(1).start()
+    for j in (2, 3):
+        cut_for(j)
+        row_copy(j).start()
+    held[col, :, row] = cut(row)
+    cut_for(5)
+    row_copy(5).start()
     for t in range(4):
         start = (rows + t // 2) * LANES
         for c in range(slab):
@@ -143,62 +198,32 @@
             else:
                 both = jnp.where(low_lane, swap(top), bottom)
             packed[t, c] = both.astype(jnp.bfloat16)
-    held[col, :, row] = blocks[row]
 
     @pl.when(owner)
     def _():
         halves[x_here, row] = packed[z_here]
 
-    pl.semaphore_wait(barrier, len(peers))
-
-    def remote(src, dst, send, recv, device):
-        return pltpu.make_async_remote_copy(
-            src_ref=src,
-            dst_ref=dst,
-            send_sem=send,
-            recv_sem=recv,
-            device_id=device,
-            device_id_type=pl.DeviceIdType.MESH,
-        )
-
-    def row_copy(j):
-        other = flip(row, j)
-        return remote(
-            blocks.at[other], held.at[col, :, row], row_send.at[j], arrive.at[col, row], at(other, col)
-        )
-
-    def extra_copy(d):
-        target = flip(z_here, d)
-        return remote(
-            packed.at[target],
-            halves.at[x_here, row],
-            extra_send.at[d],
-            arrive.at[4 + x_here, row],
-            at(2 * target + core, col),
-        )
-
-    def forward(slot, source, device, send):
-        return remote(held.at[slot, :, source], held.at[slot, :, source], send, arrive.at[slot, source], device)
-
-    def forward_half(x, source, device, send):
-        return remote(halves.at[x, source], halves.at[x, source], send, arrive.at[4 + x, source], device)
-
-    def landed(slot, source):
-        forward(slot, source, at(row, side), side_send.at[slot, source]).wait_recv()
-
-    def landed_half(x, source):
-        forward_half(x, source, at(row, side), side_send.at[4 + x, source]).wait_recv()
-
-    for j in (4, 1, 2, 3):
-        row_copy(j).start()
-
     @pl.when(jnp.logical_not(owner))
     def _():
         extra_copy(0).start()
 
     extra_copy(1).start()
-    row_copy(5).start()
     extra_copy(2).start()
+    cut_for(6)
+    cut_for(7)
+
+    def build_mix():
+        wide = amplitude_ref[...].astype(jnp.float32)
+        chosen = lax.broadcasted_iota(jnp.int32, wide.shape, 1) == col
+        mine = jnp.sum(jnp.where(chosen, wide, 0.0), axis=1)
+        lane = lax.broadcasted_iota(jnp.int32, (slab, slab * SUB), 1)
+        spread = jnp.zeros((slab, slab * SUB), jnp.float32)
+        for d in range(slab):
+            spread = spread + jnp.where(lane // SUB == d, mine[:, d : d + 1], 0.0)
+        square = (SUB, slab * SUB)
+        same = lax.broadcasted_iota(jnp.int32, square, 0) == lax.broadcasted_iota(jnp.int32, square, 1) % SUB
+        for c in range(slab):
+            mix_matrix[c * SUB : (c + 1) * SUB, :] = jnp.where(same, spread[c : c + 1, :], 0.0).astype(jnp.bfloat16)
 
     def mix(slot, source):
         groups = row_count // SUB
@@ -209,7 +234,7 @@
             ],
             axis=1,
         )
-        result = jnp.dot(mix_ref[...], wide, preferred_element_type=jnp.float32).astype(jnp.bfloat16)
+        result = jnp.dot(mix_matrix[...], wide, preferred_element_type=jnp.float32).astype(jnp.bfloat16)
         for j in range(groups):
             for c in range(slab):
                 mixed[slot, source, j * SUB : (j + 1) * SUB, c * LANES : (c + 1) * LANES] = result[
@@ -225,6 +250,72 @@
             held[4, c, source, :half_rows] = top.astype(jnp.bfloat16)
             held[4, c, source, half_rows:] = bottom.astype(jnp.bfloat16)
 
+    y_peer = flip(row, 1)
+    own_half = z_here // 2
+
+    def y_copy(d, half):
+        tile = flip(z_here, d)
+        return remote(
+            partial.at[tile, half, 1 - y_here],
+            y_in.at[tile, half],
+            y_send.at[tile, half],
+            y_arrive.at[tile, half],
+            at(y_peer, col),
+        )
+
+    def near_copy(stage, half):
+        return remote(
+            partial.at[flip(z_here, 3 - 2 * stage), half, y_here],
+            near_in.at[stage, half],
+            near_send.at[stage, half],
+            near_arrive.at[stage, half],
+            at(flip(row, 2), col),
+        )
+
+    def far_copy(half):
+        return remote(
+            partial.at[flip(z_here, 2), half, y_here],
+            far_in.at[half],
+            far_send.at[half],
+            far_arrive.at[half],
+            at(flip(row, 4), col),
+        )
+
+    def multiply(d, half):
+        tile = flip(z_here, d)
+
+        def add_slot(slot, inner):
+            left = jnp.concatenate(
+                [held[slot, c, pl.ds(2 * tile, 2)].reshape(2 * row_count, LANES) for c in range(slab)], axis=1
+            )
+            right = mixed[slot, pl.ds(4 * half, 4)].reshape(4 * row_count, slab * LANES)
+            product = lax.dot_general(
+                left, right, (((1,), (1,)), ((), ())), preferred_element_type=jnp.float32
+            ).reshape(2, row_count, 4 * row_count)
+
+            @pl.when(slot == 0)
+            def _():
+                partial[tile, half] = product
+
+            @pl.when(slot > 0)
+            def _():
+                partial[tile, half] += product
+
+            return inner
+
+        lax.fori_loop(0, 5, add_slot, 0)
+        y_copy(d, half).start()
+
+    def add_y(d, half):
+        tile = flip(z_here, d)
+        y_copy(d, half).wait_recv()
+        partial[tile, half, y_here] += y_in[tile, half]
+
+    def add_near(half):
+        near_copy(0, half).wait_recv()
+        partial[flip(z_here, 2), half, y_here] += near_in[0, half]
+        far_copy(half).start()
+
     def gather_step(step, carry):
         @pl.when(step < rows)
         def _():
@@ -246,6 +337,10 @@
                 forward_half(x_here, source, at(row, cross), cross_send.at[1, source]).start()
                 forward_half(x_here, source, at(row, side), side_send.at[4 + x_here, source]).start()
 
+        @pl.when(step == 0)
+        def _():
+            build_mix()
+
         @pl.when(step == 4)
         def _():
             row_copy(4).wait_send()
@@ -287,92 +382,73 @@
 
             lax.fori_loop(0, 5, mix_slot, 0)
 
+        @pl.when(step == rows - 1)
+        def _():
+            def early(d, inner):
+                multiply(d, own_half)
+                return inner
+
+            lax.fori_loop(0, 3, early, 0)
+
         return carry
 
     lax.fori_loop(0, rows + 2, gather_step, 0)
 
-    y_peer = flip(row, 1)
-
-    def tile_of(step):
-        return flip(z_here, 3 - step)
-
-    def y_copy(tile):
-        return remote(
-            partial.at[tile, 1 - y_here], y_in.at[tile], y_send.at[tile], y_arrive.at[tile], at(y_peer, col)
-        )
-
-    def near_copy(stage):
-        tile = flip(z_here, 3 - 2 * stage)
-        return remote(
-            partial.at[tile, y_here],
-            near_in.at[stage],
-            near_send.at[stage],
-            near_arrive.at[stage],
-            at(flip(row, 2), col),
-        )
-
-    def far_copy():
-        tile = flip(z_here, 2)
-        return remote(
-            partial.at[tile, y_here], far_in, far_send.at[0], far_arrive.at[0], at(flip(row, 4), col)
-        )
-
-    def reduce_step(step, carry):
-        @pl.when(step < 4)
-        def _():
-            tile = tile_of(step)
-
-            def multiply(slot, inner):
-                left = jnp.concatenate(
-                    [held[slot, c, pl.ds(2 * tile, 2)].reshape(2 * row_count, LANES) for c in range(slab)], axis=1
-                )
-                right = mixed[slot].reshape(rows * row_count, slab * LANES)
-                product = lax.dot_general(
-                    left, right, (((1,), (1,)), ((), ())), preferred_element_type=jnp.float32
-                ).reshape(2, row_count, rows * row_count)
-
-                @pl.when(slot == 0)
-                def _():
-                    partial[tile] = product
-
-                @pl.when(slot > 0)
-                def _():
-                    partial[tile] += product
-
-                return inner
-
-            lax.fori_loop(0, 5, multiply, 0)
-            y_copy(tile).start()
-
-        @pl.when(step >= 1)
-        def _():
-            tile = tile_of(step - 1)
-            y_copy(tile).wait_recv()
-            partial[tile, y_here] += y_in[tile]
-
-            @pl.when(step == 1)
-            def _():
-                near_copy(0).start()
-
-            @pl.when(step == 2)
-            def _():
-                near_copy(0).wait_recv()
-                partial[tile, y_here] += near_in[0]
-                far_copy().start()
-
-            @pl.when(step == 3)
-            def _():
-                near_copy(1).start()
+    def reduce_step(v, carry):
+        @pl.when(v < 5)
+        def _():
+            first = (5 - v) // 5
+            multiply(4 - v - first, flip(own_half, 1 - first))
+
+        @pl.when(v == 0)
+        def _():
+            add_y(0, own_half)
+            add_y(1, own_half)
+            near_copy(1, own_half).start()
+            add_y(2, own_half)
+
+        @pl.when(v == 1)
+        def _():
+            add_y(3, own_half)
+            near_copy(0, own_half).start()
+
+        @pl.when(v == 2)
+        def _():
+            add_y(3, 1 - own_half)
+            near_copy(0, 1 - own_half).start()
+            add_near(own_half)
+
+        @pl.when(v == 3)
+        def _():
+            add_y(2, 1 - own_half)
+            add_near(1 - own_half)
+
+        @pl.when(v == 4)
+        def _():
+            add_y(1, 1 - own_half)
+            near_copy(1, 1 - own_half).start()
+
+        @pl.when(v == 5)
+        def _():
+            add_y(0, 1 - own_half)
 
         return carry
 
-    lax.fori_loop(0, 5, reduce_step, 0)
-
-    near_copy(1).wait_recv()
-    far_copy().wait_recv()
-    total = partial[z_here, y_here] + near_in[1] + far_in[...]
-    residual_ref[0] = total
-    update_ref[0] = total / (first_ref[...] + second_ref[...] - pair_ref[...])
+    lax.fori_loop(0, 6, reduce_step, 0)
+
+    across = energy_ref[...]
+    here = lax.broadcasted_iota(jnp.int32, (row_count, rows * row_count), 1) == (
+        lax.broadcasted_iota(jnp.int32, (row_count, rows * row_count), 0) + row * row_count
+    )
+    down = jnp.sum(jnp.where(here, across, 0.0), axis=1, keepdims=True)
+    width = 4 * row_count
+    for half in range(2):
+        near_copy(1, half).wait_recv()
+        far_copy(half).wait_recv()
+        total = partial[z_here, half, y_here] + near_in[1, half] + far_in[half]
+        span = slice(half * width, (half + 1) * width)
+        residual_ref[0, :, span] = total
+        update_ref[0, :, span] = total / (down + across[:, span] - pair_ref[col])
 
     for j in (1, 2, 3, 6, 7):
         row_copy(j).wait_send()
@@ -398,29 +474,24 @@
         return carry
 
     lax.fori_loop(0, rows, finish, 0)
-    for step in range(4):
-        y_copy(tile_of(step)).wait_send()
-    near_copy(0).wait_send()
-    near_copy(1).wait_send()
-    far_copy().wait_send()
+    for half in range(2):
+        for d in range(4):
+            y_copy(d, half).wait_send()
+        near_copy(0, half).wait_send()
+        near_copy(1, half).wait_send()
+        far_copy(half).wait_send()
 
 
 def fused(factors, amplitudes, vir_energy, pair_energy):
     row_count, slab, aux = factors.shape
     vir = vir_energy.shape[0]
     rows = vir // row_count
-    here_row = lax.axis_index("row")
-    here_col = lax.axis_index("col")
     slabs = factors.transpose(1, 0, 2)
-    mine = lax.dynamic_index_in_dim(amplitudes, here_col, 0, keepdims=False)
-    mix = jnp.kron(mine, jnp.eye(SUB, dtype=mine.dtype))
-    first = lax.dynamic_slice_in_dim(vir_energy, here_row * row_count, row_count)[:, None]
-    pair = lax.dynamic_slice_in_dim(pair_energy, here_col, 1)[:, None]
     result = jax.ShapeDtypeStruct((1, row_count, vir), jnp.float32)
     dma = pltpu.SemaphoreType.DMA
     return pl.pallas_call(
         fused_kernel,
-        in_specs=[pl.BlockSpec(memory_space=pltpu.VMEM)] * 5,
+        in_specs=[pl.BlockSpec(memory_space=pltpu.VMEM)] * 3 + [pl.BlockSpec(memory_space=pltpu.SMEM)],
         out_specs=[pl.BlockSpec(memory_space=pltpu.VMEM)] * 2,
         out_shape=[result, result],
         scratch_shapes=[
@@ -429,21 +500,22 @@
             pltpu.VMEM((2, rows, slab, row_count // 2, LANES), jnp.bfloat16),
             pltpu.VMEM((5, slab, rows, row_count, LANES), jnp.bfloat16),
             pltpu.VMEM((5, rows, row_count, slab * LANES), jnp.bfloat16),
-            pltpu.VMEM((rows // 2, 2, row_count, vir), jnp.float32),
-            pltpu.VMEM((rows // 2, row_count, vir), jnp.float32),
-            pltpu.VMEM((2, row_count, vir), jnp.float32),
-            pltpu.VMEM((row_count, vir), jnp.float32),
+            pltpu.VMEM((slab * SUB, slab * SUB), jnp.bfloat16),
+            pltpu.VMEM((rows // 2, 2, 2, row_count, vir // 2), jnp.float32),
+            pltpu.VMEM((rows // 2, 2, row_count, vir // 2), jnp.float32),
+            pltpu.VMEM((2, 2, row_count, vir // 2), jnp.float32),
+            pltpu.VMEM((2, row_count, vir // 2), jnp.float32),
             dma((rows,)),
             dma((4,)),
             dma((6, rows)),
             dma((2, rows)),
             dma((6, rows)),
-            dma((rows // 2,)),
-            dma((rows // 2,)),
+            dma((rows // 2, 2)),
+            dma((rows // 2, 2)),
+            dma((2, 2)),
+            dma((2, 2)),
             dma((2,)),
             dma((2,)),
-            dma((1,)),
-            dma((1,)),
         ],
         compiler_params=pltpu.CompilerParams(
             collective_id=0, has_side_effects=True, vmem_limit_bytes=52 * 1024 * 1024
@@ -451,7 +523,7 @@
         cost_estimate=pl.CostEstimate(
             flops=2 * vir * vir * slab * LANES * 5, bytes_accessed=4 * factors.size, transcendentals=0
         ),
-    )(mix, slabs, first, vir_energy[None, :], pair)
+    )(amplitudes.transpose(1, 0, 2), slabs, vir_energy[None, :], pair_energy)
 
 
 def per_device(factors, amplitudes, vir_energy, pair_energy):

time: 134 us -> 123 us (0.918)
  Pallas kernels: 127 us -> 119 us
  local copies, waits for them, and re-layouts: 5.6 us -> 3.48 us
    pallas_call x1, Pallas kernels: 127 us -> 119 us  [fused(): pl.pallas_call(fused_kernel, in_specs=[pl.BlockSpec(memory_space=pltpu.VM...]
    unnamed x5 -> x6, local copies, waits for them, and re-layouts: 2.13 us -> 2.79 us
where the time goes in v4:
time: 123 us
  Pallas kernels  119 us (97%)
  local copies, waits for them, and re-layouts  3.48 us (3%)
    pallas_call x1, Pallas kernels, fused(): pl.pallas_call(fused_kernel, in_specs=[pl.BlockSpec(memory_space=pltpu.VM...  119 us
    unnamed x6, local copies, waits for them, and re-layouts  2.79 us

profile of v4, /device:TPU:0, one launch (start us, length us, event | category | flops | bytes accessed | tf_op | source)
XLA Modules:
  0.0 123.1 jit_solution(4633576389655874122)
XLA Ops:
  0.6 0.7 broadcast_in_dim.3.energy_ref
  1.3 0.0 copy-start
  1.3 0.7 copy-done
  2.0 0.0 copy-start.1
  2.0 0.7 copy-done.1
  2.7 118.9 %shard_map.59 = (f32[1,96,768]{2,1,0:T(8,128)S(1)}, f32[1,96,768]{2,1,0:T(8,128)S(1)}) custom-call(bf16[12,4,12]{2,1,0:T(4,128)(2,1)S(1)} %bitcast.2, bf16[12,96,1280]{2,1,0:T(8,128)(2,1)} %bitcast.3, f32[1,768]{1,0:T(1,128)S(1)} %broadcast_in_dim.3.energy_ref, f32[4]{0:T(128)S(1)} %copy-done.1), custom_call_target="tpu_custom_call" | custom-call | flops 9059696640 | bytes 5898240 | tf_op jit(solution)/shard_map/pallas_call | solution.py:492
  121.6 0.7 copy.8
  122.3 0.7 copy.9
Async XLA Ops:
  1.3 0.7 copy-start
  2.0 0.7 copy-start.1

commit v5 on v4

--- a/solution.py
+++ b/solution.py
@@ -341,16 +341,19 @@
         def _():
             build_mix()
 
-        @pl.when(step == 4)
-        def _():
-            row_copy(4).wait_send()
+        @pl.when(step == 2)
+        def _():
             row_copy(6).start()
             extra_copy(3).start()
 
+        @pl.when(step == 4)
+        def _():
+            row_copy(4).wait_send()
+            row_copy(7).start()
+
         @pl.when(step == 5)
         def _():
             row_copy(5).wait_send()
-            row_copy(7).start()
 
         @pl.when((step >= 1) & (step < rows + 1))
         def _():

time: 123 us -> 123 us (level)
  no operation moved by 1% of the time
where the time goes in v5:
time: 123 us
  Pallas kernels  119 us (97%)
  local copies, waits for them, and re-layouts  3.48 us (3%)
    pallas_call x1, Pallas kernels, fused(): pl.pallas_call(fused_kernel, in_specs=[pl.BlockSpec(memory_space=pltpu.VM...  119 us
    unnamed x6, local copies, waits for them, and re-layouts  2.79 us

profile of v5, /device:TPU:0, one launch (start us, length us, event | category | flops | bytes accessed | tf_op | source)
XLA Modules:
  0.0 123.2 jit_solution(2622158193691740012)
XLA Ops:
  0.6 0.7 broadcast_in_dim.3.energy_ref
  1.3 0.0 copy-start
  1.3 0.7 copy-done
  2.0 0.0 copy-start.1
  2.0 0.7 copy-done.1
  2.7 119.1 %shard_map.59 = (f32[1,96,768]{2,1,0:T(8,128)S(1)}, f32[1,96,768]{2,1,0:T(8,128)S(1)}) custom-call(bf16[12,4,12]{2,1,0:T(4,128)(2,1)S(1)} %bitcast.2, bf16[12,96,1280]{2,1,0:T(8,128)(2,1)} %bitcast.3, f32[1,768]{1,0:T(1,128)S(1)} %broadcast_in_dim.3.energy_ref, f32[4]{0:T(128)S(1)} %copy-done.1), custom_call_target="tpu_custom_call" | custom-call | flops 9059696640 | bytes 5898240 | tf_op jit(solution)/shard_map/pallas_call | solution.py:495
  121.8 0.7 copy.8
  122.5 0.7 copy.9
Async XLA Ops:
  1.3 0.7 copy-start
  2.0 0.7 copy-start.1
